TPU v7x, 32 devices: a whole 2x2x4 slice. The times are simulated.
32 devices in a mesh: fsdp: 8 (over y, x, core), tp: 4 (over z).
Axes of the slice: x: 2, y: 2, z: 4, core: 2. Of those that a mesh axis runs over, the one named last changes fastest.
Arguments:
- roll_rows: bfloat16 [256, 72, 3584], P('fsdp', None, 'tp'), may hold values from -60 to 60
- dest: int32 [256], P('fsdp'), may hold values from 0 to 255, as said below
- lengths: int32 [8, 32], P('fsdp'), may hold values from 1 to 72, 768 in all within a row
- clusters: int32 [256], P('fsdp'), may hold values from 0 to 3
- log_prob_grad: bfloat16 [6144, 3584], P('fsdp', 'tp'), may hold values from -6 to 6
- gain: bfloat16 [3584], replicated, may hold values from 0.5 to 1.5
- w_q: bfloat16 [3584, 2048], P('fsdp', 'tp'), may hold values from -1 to 1
- w_k: bfloat16 [3584, 512], P('fsdp', 'tp'), may hold values from -1 to 1
- w_v: bfloat16 [3584, 512], P('fsdp', 'tp'), may hold values from -0.09375 to 0.09375
- w_o_t: bfloat16 [3584, 2048], P('fsdp', 'tp'), may hold values from -0.125 to 0.125
Outputs:
- input_grad: bfloat16 [6144, 3584], P('fsdp', 'tp')
- grad_q: bfloat16 [3584, 2048], P('fsdp', 'tp')
- grad_k: bfloat16 [3584, 512], P('fsdp', 'tp')
- grad_v: bfloat16 [3584, 512], P('fsdp', 'tp')
- grad_o_t: bfloat16 [3584, 2048], P('fsdp', 'tp')
Inputs may be any that keep to these rules, and one draw needn't show every extreme that they name: dest is a permutation; every rollout replica hands exactly 4 completions to every learner, and every learner trains 32 completions. Each learner's 32 lengths sum to 768.
All inputs are finite; a program needn't handle non-finite values.
Results may differ from a plain program's by a relative error of at most 0.03.
Values may be sent and summed in bfloat16 or wider, within the bound.
No kernel may reach another device: no remote copies, remote signals or barrier semaphores. Data moves between devices by JAX's collectives and lax.ppermute only.
A program may use at most 128 MiB of HBM per device.

v0:
```python
import jax
import jax.numpy as jnp
from jax import lax
from jax.sharding import PartitionSpec as P

KEY_VALUE_HEADS = 4
HD = 128
QUERY_HEADS = 16
GSIZE = 16


ROPE_BASE = 1000000.0
NORM_EPSILON = 1e-06


def contract_rows(left, right):
    return lax.dot_general(
        left, right, (((0,), (0,)), ((), ())), preferred_element_type=jnp.float32
    )


def times_trans(left, right):
    return lax.dot_general(
        left, right, (((1,), (1,)), ((), ())), preferred_element_type=jnp.float32
    )


def rotary_tables(position):
    half_width = HD // 2
    frequency = ROPE_BASE ** (-(2.0 * jnp.arange(half_width, dtype=jnp.float32)) / HD)
    angles = position.astype(jnp.float32)[:, None] * frequency[None, :]
    return (jnp.cos(angles)[:, None, :], jnp.sin(angles)[:, None, :])


def rotate(values, rope_cos, rope_sin):
    half_width = values.shape[-1] // 2
    first_half = values[..., :half_width]
    second_half = values[..., half_width:]
    return jnp.concatenate(
        [
            first_half * rope_cos - second_half * rope_sin,
            second_half * rope_cos + first_half * rope_sin,
        ],
        axis=-1,
    )


def inverse_rotate(values, rope_cos, rope_sin):
    half_width = values.shape[-1] // 2
    first_half = values[..., :half_width]
    second_half = values[..., half_width:]
    return jnp.concatenate(
        [
            first_half * rope_cos + second_half * rope_sin,
            second_half * rope_cos - first_half * rope_sin,
        ],
        axis=-1,
    )


def per_device(roll_rows, dest, lengths, clusters, log_prob_grad, gain, w_q, w_k, w_v, w_o_t):
    sequence_count = dest.shape[0]
    max_len = roll_rows.shape[1]
    local_features = roll_rows.shape[2]
    per_pair = sequence_count // lax.axis_size("fsdp")
    slot_ids = jnp.arange(sequence_count, dtype=jnp.int32)
    target = dest // sequence_count
    within = dest % sequence_count
    ballots = clusters.reshape(sequence_count // GSIZE, GSIZE)
    vote_share = jnp.mean((ballots[:, :, None] == ballots[:, None, :]).astype(jnp.float32), axis=2)
    advantage = (
        (vote_share - jnp.mean(vote_share, axis=1, keepdims=True))
        .reshape(sequence_count)
        .astype(jnp.bfloat16)
    )
    same_target = target[:, None] == target[None, :]
    earlier = within[None, :] < within[:, None]
    rank_in = jnp.sum((same_target & earlier).astype(jnp.int32), axis=1)
    send_block = target * per_pair + rank_in
    source = jnp.sum(
        jnp.where(send_block[None, :] == slot_ids[:, None], slot_ids[None, :], 0), axis=1
    )
    send_rows = jnp.take(roll_rows, source, axis=0)
    send_place = jnp.take(within, source).astype(jnp.bfloat16)
    send_share = jnp.take(advantage, source)
    arrived_rows, arrived_place, arrived_share = (
        lax.all_to_all(send_rows, "fsdp", split_axis=0, concat_axis=0, tiled=True),
        lax.all_to_all(send_place, "fsdp", split_axis=0, concat_axis=0, tiled=True),
        lax.all_to_all(send_share, "fsdp", split_axis=0, concat_axis=0, tiled=True),
    )
    lengths_row = lengths.reshape(sequence_count)
    sequence_ends = jnp.cumsum(lengths_row)
    sequence_starts = sequence_ends - lengths_row
    row_count = log_prob_grad.shape[0]
    row_index = jnp.arange(row_count, dtype=jnp.int32)
    segment = jnp.sum((sequence_ends[None, :] <= row_index[:, None]).astype(jnp.int32), axis=1)
    one_hot = segment[:, None] == slot_ids[None, :]
    position = row_index - jnp.sum(jnp.where(one_hot, sequence_starts[None, :], 0), axis=1)
    holder = arrived_place.astype(jnp.int32)[None, :] == slot_ids[:, None]
    slot_of = jnp.sum(jnp.where(holder, slot_ids[None, :], 0), axis=1)
    seq_advantage = jnp.sum(
        jnp.where(holder, arrived_share.astype(jnp.float32)[None, :], 0.0), axis=1
    )
    row_slot = jnp.sum(jnp.where(one_hot, slot_of[None, :], 0), axis=1)
    row_advantage = jnp.sum(jnp.where(one_hot, seq_advantage[None, :], 0.0), axis=1)
    learner_rows = jnp.take(
        arrived_rows.reshape(sequence_count * max_len, local_features),
        row_slot * max_len + position,
        axis=0,
    )
    packed, cotangent = (
        lax.all_gather(learner_rows, "tp", axis=1, tiled=True),
        lax.all_gather(log_prob_grad, "tp", axis=1, tiled=True),
    )
    inputs_float = packed.astype(jnp.float32)
    inverse_norm = lax.rsqrt(
        jnp.mean(inputs_float * inputs_float, axis=1, keepdims=True) + NORM_EPSILON
    )
    unit_rows = inputs_float * inverse_norm
    gain_float = gain.astype(jnp.float32)
    normed = (unit_rows * gain_float).astype(jnp.bfloat16)
    rope_cos, rope_sin = rotary_tables(position)
    allowed = (segment[:, None] == segment[None, :]) & (position[None, :] <= position[:, None])
    grad_local = row_advantage[:, None] * log_prob_grad.astype(jnp.float32)
    grad_round = (row_advantage[:, None] * cotangent.astype(jnp.float32)).astype(jnp.bfloat16)
    weight_q, weight_k, weight_v, weight_o = (
        lax.all_gather(w_q, "fsdp", axis=0, tiled=True),
        lax.all_gather(w_k, "fsdp", axis=0, tiled=True),
        lax.all_gather(w_v, "fsdp", axis=0, tiled=True),
        lax.all_gather(w_o_t, "fsdp", axis=0, tiled=True),
    )
    query_lin = jnp.dot(normed, weight_q, preferred_element_type=jnp.float32)
    key_lin = jnp.dot(normed, weight_k, preferred_element_type=jnp.float32)
    value_lin = jnp.dot(normed, weight_v, preferred_element_type=jnp.float32)
    key_heads = w_k.shape[1] // HD
    queries_per_group = QUERY_HEADS // KEY_VALUE_HEADS
    query_rot = (
        rotate(query_lin.reshape(row_count, key_heads * queries_per_group, HD), rope_cos, rope_sin)
        .astype(jnp.bfloat16)
        .reshape(row_count, key_heads, queries_per_group, HD)
    )
    key_rot = rotate(key_lin.reshape(row_count, key_heads, HD), rope_cos, rope_sin).astype(
        jnp.bfloat16
    )
    value_b = value_lin.reshape(row_count, key_heads, HD).astype(jnp.bfloat16)
    scores = jnp.einsum(
        "ighd,jgd->ghij", query_rot, key_rot, preferred_element_type=jnp.float32
    ) * HD ** (-0.5)
    scores = jnp.where(allowed, scores, -1e30)
    row_max = jnp.max(scores, axis=-1, keepdims=True)
    exp_scores = jnp.where(allowed, jnp.exp(scores - row_max), 0.0)
    attn_prob = exp_scores / jnp.sum(exp_scores, axis=-1, keepdims=True)
    attn_prob_b = attn_prob.astype(jnp.bfloat16)
    attn_out = jnp.einsum(
        "ghij,jgd->ighd", attn_prob_b, value_b, preferred_element_type=jnp.float32
    )
    attn_out = attn_out.reshape(row_count, key_heads * queries_per_group * HD).astype(jnp.bfloat16)
    grad_attn = jnp.dot(grad_round, weight_o, preferred_element_type=jnp.float32).astype(
        jnp.bfloat16
    )
    grad_attn = grad_attn.reshape(row_count, key_heads, queries_per_group, HD)
    grad_prob = jnp.einsum("ighd,jgd->ghij", grad_attn, value_b, preferred_element_type=jnp.float32)
    grad_value_f = jnp.einsum(
        "ghij,ighd->jgd", attn_prob_b, grad_attn, preferred_element_type=jnp.float32
    )
    row_delta = jnp.sum(attn_prob * grad_prob, axis=-1, keepdims=True)
    grad_score = (attn_prob * (grad_prob - row_delta) * HD ** (-0.5)).astype(jnp.bfloat16)
    grad_qrot = jnp.einsum(
        "ghij,jgd->ighd", grad_score, key_rot, preferred_element_type=jnp.float32
    )
    grad_qrot = grad_qrot.reshape(row_count, key_heads * queries_per_group, HD)
    grad_krot = jnp.einsum(
        "ghij,ighd->jgd", grad_score, query_rot, preferred_element_type=jnp.float32
    )
    grad_query = (
        inverse_rotate(grad_qrot, rope_cos, rope_sin).astype(jnp.bfloat16).reshape(row_count, -1)
    )
    grad_key = (
        inverse_rotate(grad_krot, rope_cos, rope_sin).astype(jnp.bfloat16).reshape(row_count, -1)
    )
    grad_value = grad_value_f.astype(jnp.bfloat16).reshape(row_count, -1)
    grad_normed = (
        times_trans(grad_query, weight_q)
        + times_trans(grad_key, weight_k)
        + times_trans(grad_value, weight_v)
    )
    grad_hat = grad_normed * gain_float
    grad_in = inverse_norm * (
        grad_hat - unit_rows * jnp.mean(grad_hat * unit_rows, axis=1, keepdims=True)
    )
    summed_in = lax.psum_scatter(
        grad_in.astype(jnp.bfloat16), "tp", scatter_dimension=1, tiled=True
    ).astype(jnp.float32)
    input_grad = (grad_local + summed_in).astype(jnp.bfloat16)
    summed = lax.psum_scatter(
        jnp.concatenate(
            [
                contract_rows(normed, grad_query),
                contract_rows(normed, grad_key),
                contract_rows(normed, grad_value),
                contract_rows(grad_round, attn_out),
            ],
            axis=1,
        ).astype(jnp.bfloat16),
        "fsdp",
        scatter_dimension=0,
        tiled=True,
    ).astype(jnp.float32)
    q_cols = w_q.shape[1]
    k_cols = w_k.shape[1]
    grad_q = summed[:, :q_cols].astype(jnp.bfloat16)
    grad_k = summed[:, q_cols : q_cols + k_cols].astype(jnp.bfloat16)
    grad_v = summed[:, q_cols + k_cols : q_cols + 2 * k_cols].astype(jnp.bfloat16)
    grad_o_t = summed[:, q_cols + 2 * k_cols :].astype(jnp.bfloat16)
    return (input_grad, grad_q, grad_k, grad_v, grad_o_t)


def solution(mesh):
    in_specs = (
        P("fsdp", None, "tp"),
        P("fsdp"),
        P("fsdp", None),
        P("fsdp"),
        P("fsdp", "tp"),
        P(),
        P("fsdp", "tp"),
        P("fsdp", "tp"),
        P("fsdp", "tp"),
        P("fsdp", "tp"),
    )
    out_specs = (
        P("fsdp", "tp"),
        P("fsdp", "tp"),
        P("fsdp", "tp"),
        P("fsdp", "tp"),
        P("fsdp", "tp"),
    )
    return jax.shard_map(
        per_device, mesh=mesh, in_specs=in_specs, out_specs=out_specs, check_vma=False
    )
```

profile of v0, /device:TPU:0, one launch (start us, length us, event | category | flops | bytes accessed | tf_op | source)
XLA Modules:
  0.0 575.6 jit_solution(15616515960591885247)
XLA Ops:
  13.5 5.2 all-to-all-start
  18.7 5.4 gather_fusion.2
  24.1 4.6 broadcast_select_fusion
  28.7 4.7 all-to-all-start.2
  34.2 56.5 %all-to-all-done.2 = bf16[32,72,896]{2,1,0:T(8,128)(2,1)} async-done(((bf16[32,72,896]{2,1,0:T(8,128)(2,1)}), bf16[32,72,896]{2,1,0:T(8,128)(2,1)}, u32[]{:S(2)}, u32[]{:S(2)}) %all-to-all-start.2) | async-done | bytes 4128800 | tf_op jit(solution)/shard_map/all_to_all | solution.py:87
  90.7 6.3 %gather_fusion.3 = bf16[768,896]{1,0:T(8,128)(2,1)S(1)} fusion(bf16[2304,896]{1,0:T(8,128)(2,1)} %bitcast.4, s32[1024]{0:T(1024)S(1)} %pad_clamp_fusion), kind=kCustom, calls=%fused_computation.3 | custom fusion | bytes 2755584 | tf_op jit(solution)/shard_map/jit(_take)/gather | solution.py:106
  103.1 11.1 %all_gather.19 = bf16[3584,128]{1,0:T(8,128)(2,1)S(1)} all-gather(bf16[448,128]{1,0:T(8,128)(2,1)S(1)} %copy-done.11), channel_id=1, replica_groups=mesh['fsdp'=8,'tp'=4] {'fsdp'}, dimensions={0}, use_global_device_ids=true | all-gather | bytes 1032192 | tf_op jit(solution)/shard_map/all_gather | solution.py:128
  114.1 10.8 %all_gather.21 = bf16[3584,128]{1,0:T(8,128)(2,1)S(1)} all-gather(bf16[448,128]{1,0:T(8,128)(2,1)S(1)} %copy-done.12), channel_id=1, replica_groups=mesh['fsdp'=8,'tp'=4] {'fsdp'}, dimensions={0}, use_global_device_ids=true | all-gather | bytes 1032192 | tf_op jit(solution)/shard_map/all_gather | solution.py:129
  128.7 42.7 %all-gather.9.cloned.1.call-done = bf16[768,3584]{1,0:T(8,128)(2,1)} async-done(((bf16[768,896]{1,0:T(8,128)(2,1)}), bf16[768,3584]{1,0:T(8,128)(2,1)}) %all-gather.9.cloned.1.call-update) | async-done | bytes 5505040 | tf_op jit(solution)/shard_map/all_gather | solution.py:113
  171.3 7.8 %fusion.23 = bf16[768,512]{0,1:T(8,128)(2,1)} fusion(bf16[3584,512]{1,0:T(8,128)(2,1)} %all-gather.11.cloned.1.call-done, bf16[768,3584]{1,0:T(8,128)(2,1)} %all-gather.9.cloned.1.call-done, f32[768]{0:T(1024)S(1)} %select_reduce_fusion.2), kind=kOutput, calls=%fused_computation.48 | convolution fusion | flops 2827223040 | bytes 9964544 | tf_op jit(solution)/shard_map/dot_general | solution.py:158
  179.1 95.1 %all-gather.5.cloned.1.call-done = bf16[768,3584]{1,0:T(8,128)(2,1)} async-done(((bf16[768,896]{1,0:T(8,128)(2,1)}), bf16[768,3584]{1,0:T(8,128)(2,1)}) %all-gather.5.cloned.1.call-update) | async-done | bytes 5505040 | tf_op jit(solution)/shard_map/all_gather | solution.py:112
  286.4 22.4 %all-gather.7.cloned.1.call-done = bf16[3584,512]{1,0:T(8,128)(2,1)} async-done(((bf16[448,512]{1,0:T(8,128)(2,1)}), bf16[3584,512]{1,0:T(8,128)(2,1)}) %all-gather.7.cloned.1.call-update) | async-done | bytes 3670032 | tf_op jit(solution)/shard_map/all_gather | solution.py:127
  308.8 6.9 %fusion.73 = f32[768,512]{0,1:T(8,128)S(1)} fusion(bf16[768,3584]{1,0:T(8,128)(2,1)} %copy-done, bf16[3584,512]{1,0:T(8,128)(2,1)} %all-gather.7.cloned.1.call-done), kind=kOutput, calls=%fused_computation.142 | convolution fusion | flops 2818572288 | bytes 10747904 | tf_op jit(solution)/shard_map/dot_general | solution.py:132
  345.7 6.0 %fusion.53 = f32[768,3584]{1,0:T(8,128)} fusion(bf16[3584,128]{1,0:T(8,128)(2,1)S(1)} %all_gather.19, bf16[768,64]{0,1:T(8,128)(2,1)S(1)} %get-tuple-element.45, bf16[768,64]{0,1:T(8,128)(2,1)S(1)} %get-tuple-element.44), kind=kOutput, calls=%fused_computation.82 | convolution fusion | flops 705036288 | bytes 12124160 | tf_op jit(solution)/shard_map/dot_general | solution.py:23
  351.8 5.7 fusion.74
  357.5 12.6 %fusion.4 = (f32[768]{0:T(1024)S(1)}, f32[768,3584]{1,0:T(8,128)}) fusion(bf16[768,3584]{1,0:T(8,128)(2,1)S(1)} %bitcast.145, f32[768]{0:T(1024)S(1)} %add_rsqrt_fusion, f32[3584]{0:T(1024)S(1)} %convert_element_type.149, bf16[768,128]{0,1:T(8,128)(2,1)S(1)} %copy-done.10, bf16[3584,128]{1,0:T(8,128)(2,1)S(1)} %copy-done.5, f32[768,3584]{1,0:T(8,128)} %fusion.74, ...), kind=kOutput, calls=%fused_computation.10 | convolution fusion | flops 723909888 | bytes 39669760 | tf_op jit(solution)/shard_map/dot_general | solution.py:23
  370.2 8.7 %fusion.7 = bf16[768,3584]{1,0:T(8,128)(2,1)} fusion(f32[768,3584]{1,0:T(8,128)} %get-tuple-element.59, bf16[768,3584]{1,0:T(8,128)(2,1)S(1)} %bitcast.145, f32[768]{0:T(1024)S(1)} %broadcast_multiply_fusion, f32[768]{0:T(1024)S(1)} %add_rsqrt_fusion), kind=kLoop, calls=%fused_computation.13 | loop fusion | flops 16515072 | bytes 22026240 | tf_op jit(solution)/shard_map/convert_element_type | solution.py:192
  378.9 8.3 %copy.121 = bf16[768,3584]{0,1:T(8,128)(2,1)} copy(bf16[768,3584]{1,0:T(8,128)(2,1)} %fusion.7) | data formatting | bytes 11010048
  391.2 4.2 convolution_convert_fusion.2
  395.4 5.9 %convolution_convert_fusion.1 = bf16[3584,512]{0,1:T(8,128)(2,1)S(1)} fusion(bf16[768,512]{0,1:T(8,128)(2,1)S(1)} %bitcast.152, bf16[768,3584]{1,0:T(8,128)(2,1)} %copy-done), kind=kOutput, calls=%fused_computation.30 | convolution fusion | flops 2820407296 | bytes 9961472 | tf_op jit(solution)/shard_map/dot_general | solution.py:17
  408.4 4.1 pad_maximum_fusion
  412.5 12.8 %copy.123 = bf16[3584,1280]{1,0:T(8,128)(2,1)} copy(bf16[3584,1280]{0,1:T(8,128)(2,1)} %pad_maximum_fusion) | data formatting | bytes 18350080
  425.4 60.1 %reduce-scatter.7.cloned.1.call-done = bf16[896,768]{1,0:T(8,128)(2,1)} async-done(((bf16[3584,768]{1,0:T(8,128)(2,1)}), bf16[896,768]{1,0:T(8,128)(2,1)}) %reduce-scatter.7.cloned.1.call-update) | async-done | bytes 1376272
  488.8 75.7 %reduce-scatter.9.cloned.1.call-done = bf16[448,1280]{1,0:T(8,128)(2,1)} async-done(((bf16[3584,1280]{1,0:T(8,128)(2,1)}), bf16[448,1280]{1,0:T(8,128)(2,1)}) %reduce-scatter.9.cloned.1.call-update) | async-done | bytes 1146896
  (148 shorter events, 76.7 us)
Async XLA Ops:
  7.2 121.5 %all-gather.11.cloned.1.call-start = ((), (), s32[]{:S(2)}) async-start(), calls=%async_computation.8 | async-start | bytes 4128768 | tf_op jit(solution)/shard_map/all_gather | solution.py:130
  7.9 163.4 %all-gather.9.cloned.1.call-start = ((), (), s32[]{:S(2)}) async-start(), calls=%async_computation.7 | async-start | bytes 6881280 | tf_op jit(solution)/shard_map/all_gather | solution.py:113
  13.5 15.2 %all-to-all-start = ((bf16[8,4,1]{1,2,0:T(2,128)(2,1)}), bf16[8,4,1]{1,2,0:T(2,128)(2,1)S(1)}, u32[]{:S(2)}, u32[]{:S(2)}) async-start(bf16[8,4,1]{1,2,0:T(2,128)(2,1)} %copy.91), calls=%async_computation | async-start | bytes 8192 | tf_op jit(solution)/shard_map/all_to_all | solution.py:88
  28.7 62.1 %all-to-all-start.2 = ((bf16[32,72,896]{2,1,0:T(8,128)(2,1)}), bf16[32,72,896]{2,1,0:T(8,128)(2,1)}, u32[]{:S(2)}, u32[]{:S(2)}) async-start(bf16[32,72,896]{2,1,0:T(8,128)(2,1)} %broadcast_select_fusion), calls=%async_computation.2 | async-start | bytes 8257536 | tf_op jit(solution)/shard_map/all_to_all | solution.py:87
  33.4 240.9 %all-gather.5.cloned.1.call-start = ((), (), s32[]{:S(2)}) async-start(), calls=%async_computation.5 | async-start | bytes 6881280 | tf_op jit(solution)/shard_map/all_gather | solution.py:112
  90.7 12.3 %copy-start.11 = (bf16[448,128]{1,0:T(8,128)(2,1)S(1)}, bf16[448,128]{1,0:T(8,128)(2,1)}, u32[]{:S(2)}) copy-start(bf16[448,128]{1,0:T(8,128)(2,1)} %param.17) | copy-start | bytes 344068
  97.0 17.1 %copy-start.12 = (bf16[448,128]{1,0:T(8,128)(2,1)S(1)}, bf16[448,128]{1,0:T(8,128)(2,1)}, u32[]{:S(2)}) copy-start(bf16[448,128]{1,0:T(8,128)(2,1)} %param.18) | copy-start | bytes 344068
  97.0 27.9 %copy-start.13 = (bf16[3584]{0:T(1024)(128)(2,1)S(1)}, bf16[3584]{0:T(1024)(128)(2,1)}, u32[]{:S(2)}) copy-start(bf16[3584]{0:T(1024)(128)(2,1)} %param.15) | copy-start | bytes 21508
  98.4 210.4 %all-gather.7.cloned.1.call-start = ((), (), s32[]{:S(2)}) async-start(), calls=%async_computation.6 | async-start | bytes 4128768 | tf_op jit(solution)/shard_map/all_gather | solution.py:127
  99.7 25.2 %all-to-all-start.1 = ((bf16[8,4,1]{1,2,0:T(2,128)(2,1)}), bf16[8,4,1]{1,2,0:T(2,128)(2,1)S(1)}, u32[]{:S(2)}, u32[]{:S(2)}) async-start(bf16[8,4,1]{1,2,0:T(2,128)(2,1)} %copy.93), calls=%async_computation.1 | async-start | bytes 8192 | tf_op jit(solution)/shard_map/all_to_all | solution.py:89
  103.0 382.4 %reduce-scatter.7.cloned.1.call-start = ((), (), s32[]{:S(2)}) async-start(), calls=%async_computation.9 | async-start | bytes 6881280
  124.9 159.2 %copy-start.4 = (bf16[3584,128]{1,0:T(8,128)(2,1)}, bf16[3584,128]{1,0:T(8,128)(2,1)S(1)}, u32[]{:S(2)}) copy-start(bf16[3584,128]{1,0:T(8,128)(2,1)S(1)} %all_gather.21) | copy-start | bytes 2752516
  325.8 10.0 %copy-start.2 = (f32[768,768,4]{1,0,2:T(8,128)}, f32[768,768,4]{1,0,2:T(8,128)S(1)}, u32[]{:S(2)}) copy-start(f32[768,768,4]{1,0,2:T(8,128)S(1)} %get-tuple-element.55) | copy-start | bytes 28311556
  345.7 6.1 %copy-start.15 = (bf16[3584,512]{1,0:T(8,128)(2,1)S(1)}, bf16[3584,512]{1,0:T(8,128)(2,1)}, u32[]{:S(2)}) copy-start(bf16[3584,512]{1,0:T(8,128)(2,1)} %all-gather.7.cloned.1.call-done) | copy-start | bytes 11010052
  345.7 11.8 %slice-start = ((s8[5505024]{0:T(1024)(128)(4,1)}), s8[4194304]{0:T(1024)(128)(4,1)S(1)}, s32[]{:S(2)}) async-start(s8[5505024]{0:T(1024)(128)(4,1)} %bitcast.144), calls=%async_computation.11 | async-start | bytes 8388608
  351.8 5.7 copy-start.5
  351.8 5.7 copy-start.10
  387.3 177.3 %reduce-scatter.9.cloned.1.call-start = ((), (), s32[]{:S(2)}) async-start(), calls=%async_computation.10 | async-start | bytes 10321920
  387.6 13.8 %slice-start.2 = ((s8[9437184]{0:T(1024)(128)(4,1)}), s8[4194304]{0:T(1024)(128)(4,1)S(1)}, s32[]{:S(2)}) async-start(s8[9437184]{0:T(1024)(128)(4,1)} %bitcast.146), calls=%async_computation.13 | async-start | bytes 8388608
  391.2 10.2 %slice-start.3 = ((s8[9437184]{0:T(1024)(128)(4,1)}), s8[4194304]{0:T(1024)(128)(4,1)S(1)}, s32[]{:S(2)}) async-start(s8[9437184]{0:T(1024)(128)(4,1)} %bitcast.146), calls=%async_computation.14 | async-start | bytes 8388608
  395.4 6.0 %slice-start.4 = ((s8[9437184]{0:T(1024)(128)(4,1)}), s8[1048576]{0:T(1024)(128)(4,1)S(1)}, s32[]{:S(2)}) async-start(s8[9437184]{0:T(1024)(128)(4,1)} %bitcast.146), calls=%async_computation.15 | async-start | bytes 2097152
  395.4 6.0 %copy-start.18 = (bf16[768,128,1]{1,0,2:T(8,128)(2,1)S(1)}, bf16[768,128,1]{1,0,2:T(8,128)(2,1)}, u32[]{:S(2)}) copy-start(bf16[768,128,1]{1,0,2:T(8,128)(2,1)} %fusion.33) | copy-start | bytes 589828
  395.4 9.5 %slice-start.5 = ((s8[5505024]{0:T(1024)(128)(4,1)}), s8[4194304]{0:T(1024)(128)(4,1)S(1)}, s32[]{:S(2)}) async-start(s8[5505024]{0:T(1024)(128)(4,1)} %bitcast.154), calls=%async_computation.16 | async-start | bytes 8388608
  425.3 61.9 %copy-start.3 = (bf16[768,896]{1,0:T(8,128)(2,1)S(1)}, bf16[768,896]{1,0:T(8,128)(2,1)}, u32[]{:S(2)}) copy-start(bf16[768,896]{1,0:T(8,128)(2,1)} %param.14) | copy-start | bytes 4128772
  (11 other events, 37.9 us)
Sparse Core Ops, SparseCore 0:
  9.9 46.4 all-gather.10
  58.0 113.2 all-gather.8
  173.5 100.6 all-gather.4
  276.0 32.8 all-gather.6
  387.4 98.0 reduce-scatter.6
  488.9 75.5 reduce-scatter.8
where the time goes:
time: 582 us; the launch traced here: 576 us
  waiting for transfers between devices  355 us (61%)
  matrix products  78 us (13%)
  local copies, waits for them, and re-layouts  49.2 us (8%)
  other arithmetic  43.2 us (7%)
  blocking collectives  21.8 us (4%)
  between operations  15.2 us (3%)
  starting transfers between devices  13.6 us (2%)
    unnamed x8, waiting for transfers between devices  138 us
    all_gather x1, waiting for transfers between devices, per_device(): lax.all_gather(learner_rows, 'tp', axis=1, tiled=True)  95.1 us
    all_to_all x1, waiting for transfers between devices, per_device(): lax.all_to_all(send_rows, 'fsdp', split_axis=0, concat_axis=0, tiled=True)  56.5 us
    all_gather x1, waiting for transfers between devices, per_device(): lax.all_gather(log_prob_grad, 'tp', axis=1, tiled=True)  42.7 us
    unnamed x57, local copies, waits for them, and re-layouts  27.7 us
    dot_general x3, matrix products, times_trans(): lax.dot_general(left, right, (((1,), (1,)), ((), ())), preferred_element_...  24.4 us
    all_gather x1, waiting for transfers between devices, per_device(): lax.all_gather(w_q, 'fsdp', axis=0, tiled=True)  22.4 us
    dot_general x4, matrix products, contract_rows(): lax.dot_general(left, right, (((0,), (0,)), ((), ())), preferred_element_...  17.3 us
  transfers between devices with their start and end apart: 9, of which 6 were waited for; matrix products, arithmetic and copies ran while one was open for 15% of the time, Pallas kernels for 0%

commit v1 on v0

v1 whole, which is shorter than its diff:
```python
import functools

import jax
import jax.numpy as jnp
from jax import lax
from jax.experimental import pallas as pl
from jax.experimental.pallas import tpu as pltpu
from jax.sharding import PartitionSpec as P

KEY_VALUE_HEADS = 4
HD = 128
QUERY_HEADS = 16
GSIZE = 16
ROPE_BASE = 1000000.0
NORM_EPSILON = 1e-06
BLOCK = 128

UP = [(0, 1), (1, 2), (2, 3)]
DOWN = [(1, 0), (2, 1), (3, 2)]
UP_MID = [(1, 2), (2, 3)]
DOWN_MID = [(1, 0), (2, 1)]
TO_ENDS = [(2, 3), (1, 0)]
FROM_ENDS = [(3, 2), (0, 1)]
UP_IN = [(0, 1), (1, 2)]
DOWN_IN = [(3, 2), (2, 1)]


def contract_rows(left, right):
    return lax.dot_general(
        left, right, (((0,), (0,)), ((), ())), preferred_element_type=jnp.float32
    )


def times_trans(left, right):
    return lax.dot_general(
        left, right, (((1,), (1,)), ((), ())), preferred_element_type=jnp.float32
    )


def matmul(left, right):
    return jnp.dot(left, right, preferred_element_type=jnp.float32)


def line_gather(own, z):
    up1 = lax.ppermute(own, "tp", UP)
    down1 = lax.ppermute(own, "tp", DOWN)
    up2 = lax.ppermute(up1, "tp", UP_MID)
    down2 = lax.ppermute(down1, "tp", DOWN_MID)
    far2 = jnp.where(z >= 2, up2, down2)
    far3 = lax.ppermute(far2, "tp", TO_ENDS)
    near = jnp.where(z % 2 == 1, up1, down1)
    other = jnp.where(z == 1, down1, jnp.where(z == 2, up1, far3))
    return [own, near, far2, other]


def line_scatter(parts, z):
    own, near, far2, other = parts
    f32 = jnp.float32
    from_end = lax.ppermute(other, "tp", FROM_ENDS)
    total2 = (far2.astype(f32) + from_end.astype(f32)).astype(jnp.bfloat16)
    up2 = lax.ppermute(total2, "tp", UP_IN)
    down2 = lax.ppermute(total2, "tp", DOWN_IN)
    go_up = jnp.where(z == 1, other, near).astype(f32) + up2.astype(f32)
    go_down = jnp.where(z == 2, other, near).astype(f32) + down2.astype(f32)
    up3 = lax.ppermute(go_up.astype(jnp.bfloat16), "tp", UP)
    down3 = lax.ppermute(go_down.astype(jnp.bfloat16), "tp", DOWN)
    return own.astype(f32) + up3.astype(f32) + down3.astype(f32)


def attention_kernel(
    raw_ref, inv_ref, ga_ref, adv_ref, cos_ref, sin_ref, start_ref,
    dqkv_ref, dscaled_ref, out_ref, mean_ref,
    qkv_b, dk_acc, dv_acc,
):
    rows = raw_ref.shape[0]
    heads = ga_ref.shape[1] // HD
    qw = heads * HD
    scale = HD ** (-0.5)
    bf16 = jnp.bfloat16
    zeros = jnp.zeros((BLOCK, HD), jnp.float32)
    qkv_b[pl.ds(0, BLOCK), :] = jnp.zeros((BLOCK, qkv_b.shape[1]), bf16)
    dk_acc[pl.ds(0, BLOCK), :] = zeros
    dv_acc[pl.ds(0, BLOCK), :] = zeros

    def turn(value, cos, sin):
        return value * cos + pltpu.roll(value, HD // 2, 1) * sin

    def step(block, carry):
        base = pl.multiple_of(block * BLOCK, BLOCK)
        here = pl.ds(base, BLOCK)
        after = pl.ds(base + BLOCK, BLOCK)
        both = pl.ds(base, 2 * BLOCK)
        cos, sin = cos_ref[here, :], sin_ref[here, :]
        inv = inv_ref[here, :]
        for h in range(heads + 1):
            cols = slice(h * HD, (h + 1) * HD)
            qkv_b[after, cols] = turn(raw_ref[here, cols] * inv, cos, sin).astype(bf16)
        cols = slice(qw + HD, qw + 2 * HD)
        qkv_b[after, cols] = (raw_ref[here, cols] * inv).astype(bf16)
        dk_acc[after, :] = zeros
        dv_acc[after, :] = zeros
        adv = adv_ref[here, :]
        qs = jnp.concatenate(
            [qkv_b[after, h * HD : (h + 1) * HD] for h in range(heads)], axis=0
        )
        gs = jnp.concatenate(
            [(ga_ref[here, h * HD : (h + 1) * HD] * adv).astype(bf16) for h in range(heads)], axis=0
        )
        ks = qkv_b[both, qw : qw + HD]
        vs = qkv_b[both, qw + HD : qw + 2 * HD]
        start = start_ref[here, :] - (base - BLOCK)
        col = lax.broadcasted_iota(jnp.int32, (BLOCK, 2 * BLOCK), 1)
        row = lax.broadcasted_iota(jnp.int32, (BLOCK, 2 * BLOCK), 0) + BLOCK
        allowed = (col >= start) & (col <= row)
        bias = jnp.where(allowed, 0.0, -1e30)
        bias = jnp.concatenate([bias] * heads, axis=0)
        scores = times_trans(qs, ks) * scale + bias
        top = jnp.max(scores, axis=-1, keepdims=True)
        weight = jnp.exp(scores - top)
        prob = weight / jnp.sum(weight, axis=-1, keepdims=True)
        prob_b = prob.astype(bf16)
        out = matmul(prob_b, vs)
        grad_prob = times_trans(gs, vs)
        delta = jnp.sum(prob * grad_prob, axis=-1, keepdims=True)
        ds = (prob * (grad_prob - delta) * scale).astype(bf16)
        dq = matmul(ds, ks)
        dk_acc[both, :] += contract_rows(ds, qs)
        dv_acc[both, :] += contract_rows(prob_b, gs)
        partial = jnp.zeros((BLOCK, 1), jnp.float32)
        for h in range(heads):
            cols = slice(h * HD, (h + 1) * HD)
            part = slice(h * BLOCK, (h + 1) * BLOCK)
            out_ref[here, cols] = (out[part, :].astype(bf16).astype(jnp.float32) * adv).astype(bf16)
            grad = turn(dq[part, :], cos, -sin).astype(bf16)
            dqkv_ref[here, cols] = grad
            grad = grad.astype(jnp.float32) * inv
            dscaled_ref[here, cols] = grad.astype(bf16)
            partial += jnp.sum(grad * raw_ref[here, cols], axis=-1, keepdims=True)
        mean_ref[here, :] = partial
        return carry

    lax.fori_loop(0, rows // BLOCK, step, 0)

    def finish(block, carry):
        base = pl.multiple_of(block * BLOCK, BLOCK)
        here = pl.ds(base, BLOCK)
        after = pl.ds(base + BLOCK, BLOCK)
        cos, sin = cos_ref[here, :], sin_ref[here, :]
        inv = inv_ref[here, :]
        total = mean_ref[here, :]
        for place, grad in (
            (qw, turn(dk_acc[after, :], cos, -sin)),
            (qw + HD, dv_acc[after, :]),
        ):
            cols = slice(place, place + HD)
            grad = grad.astype(bf16)
            dqkv_ref[here, cols] = grad
            grad = grad.astype(jnp.float32) * inv
            dscaled_ref[here, cols] = grad.astype(bf16)
            total += jnp.sum(grad * raw_ref[here, cols], axis=-1, keepdims=True)
        mean_ref[here, :] = total
        return carry

    lax.fori_loop(0, rows // BLOCK, finish, 0)


def attention(raw, inv, ga, adv, cos, sin, start):
    rows, width = raw.shape
    qw = ga.shape[1]
    vmem = pl.BlockSpec(memory_space=pltpu.VMEM)
    return pl.pallas_call(
        attention_kernel,
        out_shape=(
            jax.ShapeDtypeStruct((rows, width), jnp.bfloat16),
            jax.ShapeDtypeStruct((rows, width), jnp.bfloat16),
            jax.ShapeDtypeStruct((rows, qw), jnp.bfloat16),
            jax.ShapeDtypeStruct((rows, 1), jnp.float32),
        ),
        in_specs=[vmem] * 7,
        out_specs=[vmem] * 4,
        scratch_shapes=[
            pltpu.VMEM((rows + BLOCK, width), jnp.bfloat16),
            pltpu.VMEM((rows + BLOCK, HD), jnp.float32),
            pltpu.VMEM((rows + BLOCK, HD), jnp.float32),
        ],
        compiler_params=pltpu.CompilerParams(vmem_limit_bytes=40 * 1024 * 1024),
        cost_estimate=pl.CostEstimate(
            flops=rows * 2 * BLOCK * HD * 12 * (qw // HD),
            bytes_accessed=rows * width * 8 + rows * qw * 6,
            transcendentals=rows * 2 * BLOCK * (qw // HD),
        ),
        name="attention",
    )(raw, inv, ga, adv, cos, sin, start)


def per_device(roll_rows, dest, lengths, clusters, log_prob_grad, gain, w_q, w_k, w_v, w_o_t):
    sequence_count = dest.shape[0]
    max_len, local_features = roll_rows.shape[1:]
    row_count = log_prob_grad.shape[0]
    replicas = lax.axis_size("fsdp")
    per_pair = sequence_count // replicas
    me = lax.axis_index("fsdp")
    z = lax.axis_index("tp")
    f32, bf16 = jnp.float32, jnp.bfloat16
    q_cols, k_cols = w_q.shape[1], w_k.shape[1]
    qkv_cols = q_cols + 2 * k_cols
    feature_count = gain.shape[0]

    g_parts = line_gather(log_prob_grad, z)

    slot_ids = jnp.arange(sequence_count, dtype=jnp.int32)
    earlier_dest = dest[None, :] < dest[:, None]
    send_block = jnp.sum(earlier_dest.astype(jnp.int32), axis=1)
    source = jnp.sum(
        jnp.where(send_block[None, :] == slot_ids[:, None], slot_ids[None, :], 0), axis=1
    )
    send_rows = jnp.take(roll_rows, source, axis=0, mode="clip")
    arrived_rows = lax.all_to_all(send_rows, "fsdp", split_axis=0, concat_axis=0, tiled=True)

    meta = lax.all_gather(jnp.stack([dest, clusters]), "fsdp", axis=1, tiled=True)
    all_dest, all_clusters = meta[0], meta[1]
    ballots = all_clusters.reshape(-1, GSIZE)
    vote_share = jnp.mean((ballots[:, :, None] == ballots[:, None, :]).astype(f32), axis=2)
    advantage = (
        (vote_share - jnp.mean(vote_share, axis=1, keepdims=True)).reshape(-1).astype(bf16)
    ).astype(f32)
    mine = (all_dest // sequence_count) == me
    within = all_dest % sequence_count
    of_replica = within.reshape(replicas, sequence_count)
    mine_of = mine.reshape(replicas, sequence_count)
    rank = jnp.sum(
        (mine_of[:, None, :] & (of_replica[:, None, :] < of_replica[:, :, None])).astype(jnp.int32),
        axis=2,
    )
    arrival = (jnp.arange(replicas, dtype=jnp.int32)[:, None] * per_pair + rank).reshape(-1)
    holder = mine[None, :] & (within[None, :] == slot_ids[:, None])
    slot_of = jnp.sum(jnp.where(holder, arrival[None, :], 0), axis=1)
    seq_advantage = jnp.sum(jnp.where(holder, advantage[None, :], 0.0), axis=1)

    lengths_row = lengths.reshape(sequence_count)
    sequence_ends = jnp.cumsum(lengths_row)
    sequence_starts = sequence_ends - lengths_row
    row_index = jnp.arange(row_count, dtype=jnp.int32)
    one_hot = (sequence_ends[None, :] > row_index[:, None]) & (
        sequence_starts[None, :] <= row_index[:, None]
    )
    row_start = jnp.sum(jnp.where(one_hot, sequence_starts[None, :], 0), axis=1)
    position = row_index - row_start
    row_slot = jnp.sum(jnp.where(one_hot, slot_of[None, :], 0), axis=1)
    adv = jnp.sum(jnp.where(one_hot, seq_advantage[None, :], 0.0), axis=1)[:, None]
    half_width = HD // 2
    frequency = ROPE_BASE ** (-(2.0 * jnp.arange(half_width, dtype=f32)) / HD)
    angles = position.astype(f32)[:, None] * frequency[None, :]
    cos, sin = jnp.cos(angles), jnp.sin(angles)
    cos = jnp.concatenate([cos, cos], axis=1)
    sin = jnp.concatenate([-sin, sin], axis=1)

    weights = lax.all_gather(
        jnp.concatenate([w_q, w_k, w_v, w_o_t], axis=1), "fsdp", axis=0, tiled=True
    ).reshape(4, local_features, -1)

    x_own = jnp.take(
        arrived_rows.reshape(sequence_count * max_len, local_features),
        row_slot * max_len + position,
        axis=0,
        mode="clip",
    )
    x_parts = line_gather(x_own, z)

    gain_parts = gain.astype(f32).reshape(4, local_features)
    w_parts = [lax.dynamic_index_in_dim(weights, z ^ k, 0, keepdims=False) for k in range(4)]
    gain_k = [lax.dynamic_index_in_dim(gain_parts, z ^ k, 0, keepdims=False) for k in range(4)]

    ga = sum(matmul(g_parts[k], w_parts[k][:, qkv_cols:]) for k in range(4))
    raw = sum(
        matmul((x_parts[k].astype(f32) * gain_k[k][None, :]).astype(bf16), w_parts[k][:, :qkv_cols])
        for k in range(4)
    )
    squares = sum(
        jnp.sum(jnp.square(x_parts[k].astype(f32)), axis=1, keepdims=True) for k in range(4)
    )
    inv = lax.rsqrt(squares / feature_count + NORM_EPSILON)

    dqkv, dscaled, out_scaled, row_sum = attention(
        raw, inv, ga, adv, cos, sin, row_start[:, None]
    )

    pull = inv * inv * row_sum / feature_count
    dx_parts = [
        (
            inv * (times_trans(dqkv, w_parts[k][:, :qkv_cols]) * gain_k[k][None, :])
            - x_parts[k].astype(f32) * pull
        ).astype(bf16)
        for k in range(4)
    ]
    dx = line_scatter(dx_parts, z)
    input_grad = (adv * log_prob_grad.astype(f32) + dx).astype(bf16)

    terms = jnp.zeros((4, local_features, qkv_cols + q_cols), bf16)
    for k in range(4):
        term = jnp.concatenate(
            [
                contract_rows(x_parts[k], dscaled) * gain_k[k][:, None],
                contract_rows(g_parts[k], out_scaled),
            ],
            axis=1,
        ).astype(bf16)
        terms = lax.dynamic_update_index_in_dim(terms, term, z ^ k, 0)
    summed = lax.psum_scatter(
        terms.reshape(feature_count, qkv_cols + q_cols), "fsdp", scatter_dimension=0, tiled=True
    )
    grad_q = summed[:, :q_cols]
    grad_k = summed[:, q_cols : q_cols + k_cols]
    grad_v = summed[:, q_cols + k_cols : qkv_cols]
    grad_o_t = summed[:, qkv_cols:]
    return (input_grad, grad_q, grad_k, grad_v, grad_o_t)


def solution(mesh):
    in_specs = (
        P("fsdp", None, "tp"),
        P("fsdp"),
        P("fsdp", None),
        P("fsdp"),
        P("fsdp", "tp"),
        P(),
        P("fsdp", "tp"),
        P("fsdp", "tp"),
        P("fsdp", "tp"),
        P("fsdp", "tp"),
    )
    out_specs = (
        P("fsdp", "tp"),
        P("fsdp", "tp"),
        P("fsdp", "tp"),
        P("fsdp", "tp"),
        P("fsdp", "tp"),
    )
    return jax.shard_map(
        per_device, mesh=mesh, in_specs=in_specs, out_specs=out_specs, check_vma=False
    )
```

time: 582 us -> 470 us (0.81)
  waiting for transfers between devices: 355 us -> 214 us
  matrix products: 78 us -> 39.6 us
  blocking collectives: 21.8 us -> 59.5 us
  starting transfers between devices: 13.6 us -> 44.7 us
  other arithmetic: 43.2 us -> 26.7 us
  Pallas kernels: 0 us -> 10.6 us
    ppermute x0 -> x15, waiting for transfers between devices: none -> 213 us  [the longest x2 51.5 us: line_gather(): far3 = lax.ppermute(far2, 'tp', TO_ENDS)]
    all_gather x4 -> x1, waiting for transfers between devices: 160 us -> 0.02 us  [per_device(): lax.all_gather(jnp.concatenate([w_q, w_k, w_v, w_o_t], axis=1), 'fsdp', a...]
    unnamed x8 -> x2, waiting for transfers between devices: 138 us -> 0.03 us
    all_to_all x1, waiting for transfers between devices: 56.5 us -> 0.01 us  [per_device(): lax.all_to_all(send_rows, 'fsdp', split_axis=0, concat_axis=0, tiled=True)]
    ppermute x0 -> x15, starting transfers between devices: none -> 39.3 us  [the longest x2 11.1 us: line_gather(): up1 = lax.ppermute(own, 'tp', UP)]
    all_gather x2 -> x1, blocking collectives: 21.8 us -> 59.5 us  [per_device(): lax.all_gather(jnp.stack([dest, clusters]), 'fsdp', axis=1, tiled=True)]
    dot_general x10 -> x8, matrix products: 36.4 us -> 12.4 us  [matmul(): return jnp.dot(left, right, preferred_element_type=jnp.float32)]
    unnamed x57 -> x85, local copies, waits for them, and re-layouts: 27.7 us -> 5.65 us
  transfers between devices with their start and end apart: 9 -> 18, of which waited for: 6 -> 9; matrix products, arithmetic and copies ran while one was open for 15% -> 8% of each run, Pallas kernels for 0% -> 0%
where the time goes in v1:
time: 470 us; the launch traced here: 464 us
  waiting for transfers between devices  214 us (46%)
  blocking collectives  59.5 us (13%)
  local copies, waits for them, and re-layouts  53.9 us (11%)
  starting transfers between devices  44.7 us (10%)
  matrix products  39.6 us (8%)
  other arithmetic  26.7 us (6%)
  between operations  15.4 us (3%)
  Pallas kernels  10.6 us (2%)
    all_gather x1, blocking collectives, per_device(): lax.all_gather(jnp.stack([dest, clusters]), 'fsdp', axis=1, tiled=True)  59.5 us
    ppermute x2, waiting for transfers between devices, line_gather(): far3 = lax.ppermute(far2, 'tp', TO_ENDS)  51.5 us
    ppermute x2, waiting for transfers between devices, line_gather(): down2 = lax.ppermute(down1, 'tp', DOWN_MID)  50.5 us
    ppermute x1, waiting for transfers between devices, line_scatter(): from_end = lax.ppermute(other, 'tp', FROM_ENDS)  29 us
    ppermute x1, waiting for transfers between devices, line_scatter(): up2 = lax.ppermute(total2, 'tp', UP_IN)  26.7 us
    ppermute x1, waiting for transfers between devices, line_scatter(): up3 = lax.ppermute(go_up.astype(jnp.bfloat16), 'tp', UP)  25.7 us
    ppermute x2, waiting for transfers between devices, line_gather(): down1 = lax.ppermute(own, 'tp', DOWN)  25 us
    dot_general x8, matrix products, contract_rows(): lax.dot_general(left, right, (((0,), (0,)), ((), ())), preferred_element_...  17.9 us
  transfers between devices with their start and end apart: 18, of which 9 were waited for; matrix products, arithmetic and copies ran while one was open for 8% of the time, Pallas kernels for 0%

profile of v1, /device:TPU:0, one launch (start us, length us, event | category | flops | bytes accessed | tf_op | source)
XLA Modules:
  0.0 463.8 jit_solution(1114841640657927668)
XLA Ops:
  9.9 5.3 %gather_fusion = bf16[32,72,896]{2,1,0:T(8,128)(2,1)} fusion(bf16[32,72,896]{2,1,0:T(8,128)(2,1)} %param.10, s32[1024]{0:T(1024)S(1)} %pad_clamp_fusion.1), kind=kCustom, calls=%fused_computation | custom fusion | bytes 8257664 | tf_op jit(solution)/shard_map/jit(_take)/gather | solution.py:217
  15.2 5.3 %all-to-all-start = ((bf16[32,72,896]{2,1,0:T(8,128)(2,1)}), bf16[32,72,896]{2,1,0:T(8,128)(2,1)}, u32[]{:S(2)}, u32[]{:S(2)}) async-start(bf16[32,72,896]{2,1,0:T(8,128)(2,1)} %gather_fusion), calls=%async_computation | async-start | bytes 8257536 | tf_op jit(solution)/shard_map/all_to_all | solution.py:218
  20.6 5.5 %collective-permute-start.5 = (bf16[768,896]{1,0:T(8,128)(2,1)S(1)}, bf16[768,896]{1,0:T(8,128)(2,1)}, u32[]{:S(2)}, u32[]{:S(2)}) collective-permute-start(bf16[768,896]{1,0:T(8,128)(2,1)S(1)} %copy-done.38), channel_id=1, source_target_pairs={{0,1},{1,2},{2,3},{4,5},{5,6},{6,7},{8,9},{9,10},{10,11},{12,13},{... | collective-permute-start | bytes 4128776 | tf_op jit(solution)/shard_map/ppermute | solution.py:45
  27.3 59.5 %all-gather = s32[8,32,2]{1,2,0:T(2,128)S(1)} all-gather(s32[1,32,2]{1,2,0:T(2,128)S(1)} %add_bitcast_fusion), channel_id=1, replica_groups=mesh['fsdp'=8,'tp'=4] {'fsdp'}, dimensions={0}, use_global_device_ids=true | all-gather | bytes 2304 | tf_op jit(solution)/shard_map/all_gather | solution.py:220
  88.1 6.2 %gather_fusion.1 = bf16[768,896]{1,0:T(8,128)(2,1)S(1)} fusion(bf16[2304,896]{1,0:T(8,128)(2,1)} %bitcast.8, s32[1024]{0:T(1024)S(1)} %pad_clamp_fusion), kind=kCustom, calls=%fused_computation.1 | custom fusion | bytes 2755584 | tf_op jit(solution)/shard_map/jit(_take)/gather | solution.py:262
  95.6 5.6 %collective-permute-start = (bf16[768,896]{1,0:T(8,128)(2,1)S(1)}, bf16[768,896]{1,0:T(8,128)(2,1)}, u32[]{:S(2)}, u32[]{:S(2)}) collective-permute-start(bf16[768,896]{1,0:T(8,128)(2,1)S(1)} %gather_fusion.1), channel_id=1, source_target_pairs={{0,1},{1,2},{2,3},{4,5},{5,6},{6,7},{8,9},{9,10},{10,11},{12,13},{... | collective-permute-start | bytes 4128776 | tf_op jit(solution)/shard_map/ppermute | solution.py:45
  104.3 25.0 %collective-permute-done.1 = bf16[768,896]{1,0:T(8,128)(2,1)} collective-permute-done((bf16[768,896]{1,0:T(8,128)(2,1)S(1)}, bf16[768,896]{1,0:T(8,128)(2,1)}, u32[]{:S(2)}, u32[]{:S(2)}) %collective-permute-start.1) | collective-permute-done | bytes 1376288 | tf_op jit(solution)/shard_map/ppermute | solution.py:46
  133.1 25.7 %collective-permute-done.8 = bf16[768,896]{1,0:T(8,128)(2,1)} collective-permute-done((bf16[768,896]{1,0:T(8,128)(2,1)}, bf16[768,896]{1,0:T(8,128)(2,1)}, u32[]{:S(2)}, u32[]{:S(2)}) %collective-permute-start.8) | collective-permute-done | bytes 1376288 | tf_op jit(solution)/shard_map/ppermute | solution.py:48
  163.4 24.8 %collective-permute-done.3 = bf16[768,896]{1,0:T(8,128)(2,1)S(1)} collective-permute-done((bf16[768,896]{1,0:T(8,128)(2,1)}, bf16[768,896]{1,0:T(8,128)(2,1)S(1)}, u32[]{:S(2)}, u32[]{:S(2)}) %collective-permute-start.3) | collective-permute-done | bytes 1376288 | tf_op jit(solution)/shard_map/ppermute | solution.py:48
  192.4 25.3 %collective-permute-done.9 = bf16[768,896]{1,0:T(8,128)(2,1)} collective-permute-done((bf16[768,896]{1,0:T(8,128)(2,1)}, bf16[768,896]{1,0:T(8,128)(2,1)}, u32[]{:S(2)}, u32[]{:S(2)}) %collective-permute-start.9) | collective-permute-done | bytes 1376288 | tf_op jit(solution)/shard_map/ppermute | solution.py:50
  220.4 26.2 %collective-permute-done.4 = bf16[768,896]{1,0:T(8,128)(2,1)S(1)} collective-permute-done((bf16[768,896]{1,0:T(8,128)(2,1)S(1)}, bf16[768,896]{1,0:T(8,128)(2,1)S(1)}, u32[]{:S(2)}, u32[]{:S(2)}) %collective-permute-start.4) | collective-permute-done | bytes 1376288 | tf_op jit(solution)/shard_map/ppermute | solution.py:50
  246.6 4.3 fusion.4
  251.1 4.4 dynamic-slice_bitcast_fusion.1
  270.7 10.6 %attention.1 = (bf16[768,768]{1,0:T(8,128)(2,1)S(1)}, bf16[768,768]{1,0:T(8,128)(2,1)S(1)}, bf16[768,512]{1,0:T(8,128)(2,1)S(1)}, f32[768,1]{1,0:T(8,128)S(1)}) custom-call(f32[768,768]{1,0:T(8,128)S(1)} %add_add_fusion.raw_ref, f32[768,1]{1,0:T(8,128)S(1)} %reshape.421.inv_ref, f32[768,512]{1,0:T(8,128)S(1)} %fusion.17.ga_ref, ...), custom_call_target="tpu_custom_call" | custom-call | flops 1207959552 | bytes 7077888 | tf_op jit(solution)/shard_map/attention/pallas_call | solution.py:171
  298.4 4.3 copy.56
  306.7 4.2 copy.54
  313.9 4.2 copy.55
  321.1 4.4 copy.53
  344.3 29.0 %collective-permute-done.10 = bf16[768,896]{1,0:T(8,128)(2,1)S(1)} collective-permute-done((bf16[768,896]{1,0:T(8,128)(2,1)S(1)}, bf16[768,896]{1,0:T(8,128)(2,1)S(1)}, u32[]{:S(2)}, u32[]{:S(2)}) %collective-permute-start.10) | collective-permute-done | bytes 1376288 | tf_op jit(solution)/shard_map/ppermute | solution.py:59
  375.7 5.0 %collective-permute-start.11 = (bf16[768,896]{1,0:T(8,128)(2,1)S(1)}, bf16[768,896]{1,0:T(8,128)(2,1)S(1)}, u32[]{:S(2)}, u32[]{:S(2)}) collective-permute-start(bf16[768,896]{1,0:T(8,128)(2,1)S(1)} %add_convert_fusion.3), channel_id=1, source_target_pairs={{0,1},{1,2},{4,5},{5,6},{8,9},{9,10},{12,13},{13,14},{16,17},{17,1... | collective-permute-start | bytes 4128776 | tf_op jit(solution)/shard_map/ppermute | solution.py:61
  382.3 26.7 %collective-permute-done.11 = bf16[768,896]{1,0:T(8,128)(2,1)S(1)} collective-permute-done((bf16[768,896]{1,0:T(8,128)(2,1)S(1)}, bf16[768,896]{1,0:T(8,128)(2,1)S(1)}, u32[]{:S(2)}, u32[]{:S(2)}) %collective-permute-start.11) | collective-permute-done | bytes 1376288 | tf_op jit(solution)/shard_map/ppermute | solution.py:61
  409.8 7.9 %collective-permute-start.12 = (bf16[768,896]{1,0:T(8,128)(2,1)S(1)}, bf16[768,896]{1,0:T(8,128)(2,1)S(1)}, u32[]{:S(2)}, u32[]{:S(2)}) collective-permute-start(bf16[768,896]{1,0:T(8,128)(2,1)S(1)} %get-tuple-element.33), channel_id=1, source_target_pairs={{0,1},{1,2},{2,3},{4,5},{5,6},{6,7},{8,9},{9,10},{10,11},{12,13},{... | collective-permute-start | bytes 4128776 | tf_op jit(solution)/shard_map/ppermute | solution.py:65
  419.0 25.7 %collective-permute-done.12 = bf16[768,896]{1,0:T(8,128)(2,1)S(1)} collective-permute-done((bf16[768,896]{1,0:T(8,128)(2,1)S(1)}, bf16[768,896]{1,0:T(8,128)(2,1)S(1)}, u32[]{:S(2)}, u32[]{:S(2)}) %collective-permute-start.12) | collective-permute-done | bytes 1376288 | tf_op jit(solution)/shard_map/ppermute | solution.py:65
  444.7 5.0 %collective-permute-done.14 = bf16[768,896]{1,0:T(8,128)(2,1)S(1)} collective-permute-done((bf16[768,896]{1,0:T(8,128)(2,1)S(1)}, bf16[768,896]{1,0:T(8,128)(2,1)S(1)}, u32[]{:S(2)}, u32[]{:S(2)}) %collective-permute-start.14) | collective-permute-done | bytes 1376288 | tf_op jit(solution)/shard_map/ppermute | solution.py:66
  (190 shorter events, 98.3 us)
Async XLA Ops:
  7.2 243.9 %all-gather.3.cloned.1.call-start = ((), (), s32[]{:S(2)}) async-start(), calls=%async_computation.2 | async-start | bytes 10321920 | tf_op jit(solution)/shard_map/all_gather | solution.py:258
  15.2 72.3 %copy-start.35 = (s32[1,32]{1,0:T(1,128)S(1)}, s32[1,32]{1,0:T(1,128)}, u32[]{:S(2)}) copy-start(s32[1,32]{1,0:T(1,128)} %param.12) | copy-start | bytes 388
  15.2 72.9 %all-to-all-start = ((bf16[32,72,896]{2,1,0:T(8,128)(2,1)}), bf16[32,72,896]{2,1,0:T(8,128)(2,1)}, u32[]{:S(2)}, u32[]{:S(2)}) async-start(bf16[32,72,896]{2,1,0:T(8,128)(2,1)} %gather_fusion), calls=%async_computation | async-start | bytes 8257536 | tf_op jit(solution)/shard_map/all_to_all | solution.py:218
  20.5 432.2 %reduce-scatter.2.cloned.1.call-start = ((), (), s32[]{:S(2)}) async-start(), calls=%async_computation.3 | async-start | bytes 10321920 | tf_op jit(solution)/shard_map/reduce_scatter | solution.py:309
  20.6 80.7 %collective-permute-start.5 = (bf16[768,896]{1,0:T(8,128)(2,1)S(1)}, bf16[768,896]{1,0:T(8,128)(2,1)}, u32[]{:S(2)}, u32[]{:S(2)}) collective-permute-start(bf16[768,896]{1,0:T(8,128)(2,1)S(1)} %copy-done.38), channel_id=1, source_target_pairs={{0,1},{1,2},{2,3},{4,5},{5,6},{6,7},{8,9},{9,10},{10,11},{12,13},{... | collective-permute-start | bytes 4128776 | tf_op jit(solution)/shard_map/ppermute | solution.py:45
  26.0 77.0 %collective-permute-start.6 = (bf16[768,896]{1,0:T(8,128)(2,1)S(1)}, bf16[768,896]{1,0:T(8,128)(2,1)}, u32[]{:S(2)}, u32[]{:S(2)}) collective-permute-start(bf16[768,896]{1,0:T(8,128)(2,1)S(1)} %copy-done.38), channel_id=1, source_target_pairs={{1,0},{2,1},{3,2},{5,4},{6,5},{7,6},{9,8},{10,9},{11,10},{13,12},{... | collective-permute-start | bytes 4128776 | tf_op jit(solution)/shard_map/ppermute | solution.py:46
  94.3 35.0 %collective-permute-start.1 = (bf16[768,896]{1,0:T(8,128)(2,1)S(1)}, bf16[768,896]{1,0:T(8,128)(2,1)}, u32[]{:S(2)}, u32[]{:S(2)}) collective-permute-start(bf16[768,896]{1,0:T(8,128)(2,1)S(1)} %gather_fusion.1), channel_id=1, source_target_pairs={{1,0},{2,1},{3,2},{5,4},{6,5},{7,6},{9,8},{10,9},{11,10},{13,12},{... | collective-permute-start | bytes 4128776 | tf_op jit(solution)/shard_map/ppermute | solution.py:46
  95.6 35.0 %collective-permute-start = (bf16[768,896]{1,0:T(8,128)(2,1)S(1)}, bf16[768,896]{1,0:T(8,128)(2,1)}, u32[]{:S(2)}, u32[]{:S(2)}) collective-permute-start(bf16[768,896]{1,0:T(8,128)(2,1)S(1)} %gather_fusion.1), channel_id=1, source_target_pairs={{0,1},{1,2},{2,3},{4,5},{5,6},{6,7},{8,9},{9,10},{10,11},{12,13},{... | collective-permute-start | bytes 4128776 | tf_op jit(solution)/shard_map/ppermute | solution.py:45
  101.2 31.8 %collective-permute-start.7 = (bf16[768,896]{1,0:T(8,128)(2,1)}, bf16[768,896]{1,0:T(8,128)(2,1)}, u32[]{:S(2)}, u32[]{:S(2)}) collective-permute-start(bf16[768,896]{1,0:T(8,128)(2,1)} %collective-permute-done.5), channel_id=1, source_target_pairs={{1,2},{2,3},{5,6},{6,7},{9,10},{10,11},{13,14},{14,15},{17,18},{18... | collective-permute-start | bytes 4128776 | tf_op jit(solution)/shard_map/ppermute | solution.py:47
  103.0 55.8 %collective-permute-start.8 = (bf16[768,896]{1,0:T(8,128)(2,1)}, bf16[768,896]{1,0:T(8,128)(2,1)}, u32[]{:S(2)}, u32[]{:S(2)}) collective-permute-start(bf16[768,896]{1,0:T(8,128)(2,1)} %collective-permute-done.6), channel_id=1, source_target_pairs={{1,0},{2,1},{5,4},{6,5},{9,8},{10,9},{13,12},{14,13},{17,16},{18,1... | collective-permute-start | bytes 4128776 | tf_op jit(solution)/shard_map/ppermute | solution.py:48
  129.3 58.9 %collective-permute-start.3 = (bf16[768,896]{1,0:T(8,128)(2,1)}, bf16[768,896]{1,0:T(8,128)(2,1)S(1)}, u32[]{:S(2)}, u32[]{:S(2)}) collective-permute-start(bf16[768,896]{1,0:T(8,128)(2,1)} %collective-permute-done.1), channel_id=1, source_target_pairs={{1,0},{2,1},{5,4},{6,5},{9,8},{10,9},{13,12},{14,13},{17,16},{18,1... | collective-permute-start | bytes 4128776 | tf_op jit(solution)/shard_map/ppermute | solution.py:48
  130.6 57.6 %collective-permute-start.2 = (bf16[768,896]{1,0:T(8,128)(2,1)}, bf16[768,896]{1,0:T(8,128)(2,1)}, u32[]{:S(2)}, u32[]{:S(2)}) collective-permute-start(bf16[768,896]{1,0:T(8,128)(2,1)} %collective-permute-done), channel_id=1, source_target_pairs={{1,2},{2,3},{5,6},{6,7},{9,10},{10,11},{13,14},{14,15},{17,18},{18... | collective-permute-start | bytes 4128776 | tf_op jit(solution)/shard_map/ppermute | solution.py:47
  161.4 56.3 %collective-permute-start.9 = (bf16[768,896]{1,0:T(8,128)(2,1)}, bf16[768,896]{1,0:T(8,128)(2,1)}, u32[]{:S(2)}, u32[]{:S(2)}) collective-permute-start(bf16[768,896]{1,0:T(8,128)(2,1)} %broadcast_select_fusion), channel_id=1, source_target_pairs={{2,3},{1,0},{6,7},{5,4},{10,11},{9,8},{14,15},{13,12},{18,19},{17,... | collective-permute-start | bytes 4128776 | tf_op jit(solution)/shard_map/ppermute | solution.py:50
  163.3 97.8 %copy-start.33 = (f32[896]{0:T(1024)}, f32[896]{0:T(1024)S(1)}, u32[]{:S(2)}) copy-start(f32[896]{0:T(1024)S(1)} %get-tuple-element.14) | copy-start | bytes 10756
  163.3 99.6 %copy-start.31 = (f32[896]{0:T(1024)}, f32[896]{0:T(1024)S(1)}, u32[]{:S(2)}) copy-start(f32[896]{0:T(1024)S(1)} %get-tuple-element.15) | copy-start | bytes 10756
  188.8 57.8 %collective-permute-start.4 = (bf16[768,896]{1,0:T(8,128)(2,1)S(1)}, bf16[768,896]{1,0:T(8,128)(2,1)S(1)}, u32[]{:S(2)}, u32[]{:S(2)}) collective-permute-start(bf16[768,896]{1,0:T(8,128)(2,1)S(1)} %get-tuple-element.24), channel_id=1, source_target_pairs={{2,3},{1,0},{6,7},{5,4},{10,11},{9,8},{14,15},{13,12},{18,19},{17,... | collective-permute-start | bytes 4128776 | tf_op jit(solution)/shard_map/ppermute | solution.py:50
  342.4 30.9 %collective-permute-start.10 = (bf16[768,896]{1,0:T(8,128)(2,1)S(1)}, bf16[768,896]{1,0:T(8,128)(2,1)S(1)}, u32[]{:S(2)}, u32[]{:S(2)}) collective-permute-start(bf16[768,896]{1,0:T(8,128)(2,1)S(1)} %fusion.15), channel_id=1, source_target_pairs={{3,2},{0,1},{7,6},{4,5},{11,10},{8,9},{15,14},{12,13},{19,18},{16,... | collective-permute-start | bytes 4128776 | tf_op jit(solution)/shard_map/ppermute | solution.py:59
  375.0 7.3 %collective-permute-start.13 = (bf16[768,896]{1,0:T(8,128)(2,1)S(1)}, bf16[768,896]{1,0:T(8,128)(2,1)S(1)}, u32[]{:S(2)}, u32[]{:S(2)}) collective-permute-start(bf16[768,896]{1,0:T(8,128)(2,1)S(1)} %add_convert_fusion.3), channel_id=1, source_target_pairs={{3,2},{2,1},{7,6},{6,5},{11,10},{10,9},{15,14},{14,13},{19,18},{18... | collective-permute-start | bytes 4128776 | tf_op jit(solution)/shard_map/ppermute | solution.py:62
  375.7 33.3 %collective-permute-start.11 = (bf16[768,896]{1,0:T(8,128)(2,1)S(1)}, bf16[768,896]{1,0:T(8,128)(2,1)S(1)}, u32[]{:S(2)}, u32[]{:S(2)}) collective-permute-start(bf16[768,896]{1,0:T(8,128)(2,1)S(1)} %add_convert_fusion.3), channel_id=1, source_target_pairs={{0,1},{1,2},{4,5},{5,6},{8,9},{9,10},{12,13},{13,14},{16,17},{17,1... | collective-permute-start | bytes 4128776 | tf_op jit(solution)/shard_map/ppermute | solution.py:61
  382.2 67.5 %copy-start.14 = (bf16[768,896]{1,0:T(8,128)(2,1)S(1)}, bf16[768,896]{1,0:T(8,128)(2,1)}, u32[]{:S(2)}) copy-start(bf16[768,896]{1,0:T(8,128)(2,1)} %copy-done.11) | copy-start | bytes 4128772
  382.2 67.5 %copy-start.16 = (bf16[896,1280]{1,0:T(8,128)(2,1)S(1)}, bf16[896,1280]{1,0:T(8,128)(2,1)}, u32[]{:S(2)}) copy-start(bf16[896,1280]{1,0:T(8,128)(2,1)} %copy-done.15) | copy-start | bytes 6881284
  382.2 67.4 %copy-start.41 = (bf16[768,896]{1,0:T(8,128)(2,1)S(1)}, bf16[768,896]{1,0:T(8,128)(2,1)}, u32[]{:S(2)}) copy-start(bf16[768,896]{1,0:T(8,128)(2,1)} %param.14) | copy-start | bytes 4128772
  409.8 34.9 %collective-permute-start.12 = (bf16[768,896]{1,0:T(8,128)(2,1)S(1)}, bf16[768,896]{1,0:T(8,128)(2,1)S(1)}, u32[]{:S(2)}, u32[]{:S(2)}) collective-permute-start(bf16[768,896]{1,0:T(8,128)(2,1)S(1)} %get-tuple-element.33), channel_id=1, source_target_pairs={{0,1},{1,2},{2,3},{4,5},{5,6},{6,7},{8,9},{9,10},{10,11},{12,13},{... | collective-permute-start | bytes 4128776 | tf_op jit(solution)/shard_map/ppermute | solution.py:65
  417.7 31.9 %collective-permute-start.14 = (bf16[768,896]{1,0:T(8,128)(2,1)S(1)}, bf16[768,896]{1,0:T(8,128)(2,1)S(1)}, u32[]{:S(2)}, u32[]{:S(2)}) collective-permute-start(bf16[768,896]{1,0:T(8,128)(2,1)S(1)} %get-tuple-element.34), channel_id=1, source_target_pairs={{1,0},{2,1},{3,2},{5,4},{6,5},{7,6},{9,8},{10,9},{11,10},{13,12},{... | collective-permute-start | bytes 4128776 | tf_op jit(solution)/shard_map/ppermute | solution.py:66
  (36 other events, 373.2 us)
Sparse Core Ops, SparseCore 0:
  9.9 97.3 all-gather.2
  338.9 77.5 reduce-scatter.1
